TPU v7x, 256 devices: a whole 4x4x8 slice. The times are simulated.
256 devices in a mesh: ctx: 32 (over y, x, core), head: 8 (over z).
Axes of the slice: x: 4, y: 4, z: 8, core: 2. Of those that a mesh axis runs over, the one named last changes fastest.
Arguments:
- queries: bfloat16 [16384, 4096], P('ctx', 'head'), may hold values from -8 to 8
- keys: bfloat16 [16384, 1024], P('ctx', 'head'), may hold values from -8 to 8
- values: bfloat16 [16384, 1024], P('ctx', 'head'), may hold values from -6 to 6
- lengths: int32 [64], replicated, may hold values from 1 to 4096, 16384 in all
- out_weight: bfloat16 [4096, 4096], P(None, 'head'), may hold values from -0.09375 to 0.09375
Outputs:
- mixed: bfloat16 [16384, 4096], P('ctx', 'head')
Inputs may be any that keep to these rules, and one draw needn't show every extreme that they name: `lengths`: each document holds at least one token and one holds exactly 4096; they sum to 16384.
All inputs are finite; a program needn't handle non-finite values.
Results may differ from a plain program's by a relative error of at most 0.0085.
Values may be sent and summed in bfloat16 or wider, within the bound.
A program may use at most 64 MiB of HBM per device.

v0:
```python
import jax
import jax.numpy as jnp
from jax import lax
from jax.sharding import PartitionSpec as P

HEAD_SIZE = 128


def shifted(shard, axis, by):
    peers = lax.axis_size(axis)
    pairs = [(i, i + by) for i in range(peers) if 0 <= i + by < peers]
    return lax.ppermute(shard, axis, pairs)


def doc_labels(lengths, positions):
    boundary = jnp.cumsum(lengths)
    return jnp.sum((boundary[None, :] <= positions[:, None]).astype(jnp.int32), axis=1) + 1


def attend(softmax_state, grouped_queries, labels, key_block, value_block, key_labels, causal):
    tok_local = grouped_queries.shape[0]
    kv_local = key_block.shape[1] // HEAD_SIZE
    keyed_rows = key_block.reshape(tok_local, kv_local, HEAD_SIZE)
    valued_rows = value_block.reshape(tok_local, kv_local, HEAD_SIZE)
    scores = jnp.einsum(
        "tkgd,skd->kgts", grouped_queries, keyed_rows, preferred_element_type=jnp.float32
    ) * HEAD_SIZE ** (-0.5)
    allowed = labels[:, None] == key_labels[None, :]
    if causal:
        allowed = allowed & jnp.tril(jnp.ones((tok_local, tok_local), dtype=bool))
    scores = jnp.where(allowed, scores, -1e30)
    run_max, run_total, numer = softmax_state
    new_max = jnp.maximum(run_max, jnp.max(scores, axis=-1))
    factor = jnp.exp(run_max - new_max)
    weights = jnp.exp(scores - new_max[..., None])
    run_total = run_total * factor + jnp.sum(weights, axis=-1)
    numer = numer * factor[..., None] + jnp.einsum(
        "kgts,skd->kgtd",
        weights.astype(jnp.bfloat16),
        valued_rows,
        preferred_element_type=jnp.float32,
    )
    return (new_max, run_total, numer)


def shards(queries, keys, values, lengths, out_weight):
    tok_local = queries.shape[0]
    kv_local = keys.shape[1] // HEAD_SIZE
    query_group_size = queries.shape[1] // keys.shape[1]
    positions = lax.axis_index("ctx") * tok_local + jnp.arange(tok_local, dtype=jnp.int32)
    labels = doc_labels(lengths, positions)
    grouped_queries = queries.reshape(tok_local, kv_local, query_group_size, HEAD_SIZE)
    softmax_state = (
        jnp.full((kv_local, query_group_size, tok_local), -1e30, jnp.float32),
        jnp.zeros((kv_local, query_group_size, tok_local), jnp.float32),
        jnp.zeros((kv_local, query_group_size, tok_local, HEAD_SIZE), jnp.float32),
    )
    softmax_state = attend(softmax_state, grouped_queries, labels, keys, values, labels, True)
    reach_shards = lax.axis_size("ctx") // 4

    def visit(state_now, carried):
        return (
            attend(state_now, grouped_queries, labels, carried[0], carried[1], carried[2], False),
            None,
        )

    def turn_step(turn_index, carry):
        state_now, carried = carry
        carried = shifted((carried[0], carried[1], carried[2]), "ctx", 1)
        return (visit(state_now, carried)[0], carried)

    softmax_state, unused = lax.fori_loop(
        0, reach_shards, turn_step, (softmax_state, (keys, values, labels))
    )
    run_max, run_total, numer = softmax_state
    attended = numer / run_total[..., None]
    attended = (
        jnp.transpose(attended, (2, 0, 1, 3))
        .reshape(tok_local, queries.shape[1])
        .astype(jnp.bfloat16)
    )
    mixed = jnp.dot(
        lax.all_gather(attended, "head", axis=1, tiled=True),
        out_weight,
        preferred_element_type=jnp.float32,
    )
    return mixed.astype(jnp.bfloat16)


def solution(mesh):
    return jax.shard_map(
        shards,
        mesh=mesh,
        in_specs=(P("ctx", "head"), P("ctx", "head"), P("ctx", "head"), P(), P(None, "head")),
        out_specs=P("ctx", "head"),
        check_vma=False,
    )
```

profile of v0, /device:TPU:1, one launch (start us, length us, event | category | flops | bytes accessed | tf_op | source)
XLA Modules:
  0.0 203.0 jit_solution(10107928225188208874)
XLA Ops:
  10.9 1.9 fusion.22
  15.0 3.5 %fusion.30 = f32[1,4,512,128]{3,2,1,0:T(8,128)S(1)} fusion(f32[512,512,4]{1,0,2:T(8,128)} %copy-done, f32[4,512]{1,0:T(4,128)S(1)} %get-tuple-element.97, pred[512,512]{0,1:T(8,128)(4,1)S(1)} %fusion.33, f32[4,512]{1,0:T(4,128)S(1)} %get-tuple-element.95, bf16[512,128]{1,0:T(8,128)(2,1)S(1)} %copy.58), kind=kOutput, calls=%fused_computation.30 | convolution fusion | flops 272891904 | bytes 5652480 | tf_op jit(solution)/shard_map/kgts,skd->kgtd/dot_general | solution.py:37
  18.5 110.5 %while.20 = (s32[]{:T(128)}, f32[1,4,512]{2,1,0:T(4,128)S(1)}, f32[1,4,512]{2,1,0:T(4,128)S(1)}, f32[1,4,512,128]{3,2,1,0:T(8,128)S(1)}, bf16[512,128]{1,0:T(8,1...) while((s32[]{:T(128)}, f32[1,4,512]{2,1,0:T(4,128)S(1)}, ...), condition=%wide.region_7.8_spmd, body=%wide.region_4.7_spmd.sunk | while | flops 549197824 | bytes 18235612 | solution.py:72
  18.6 4.5 %collective-permute-start = (s32[512]{0:T(512)S(1)}, s32[512]{0:T(512)S(1)}, u32[]{:S(2)}, u32[]{:S(2)}) collective-permute-start(s32[512]{0:T(512)S(1)} %get-tuple-element.179), channel_id=1, source_target_pairs={{0,8},{8,16},{16,24},{24,32},{32,40},{40,48},{48,56},{56,64},{64,7... | collective-permute-start | bytes 6152 | tf_op jit(solution)/shard_map/while/body/eval_jaxpr/ppermute | solution.py:12
  23.1 1.9 collective-permute-start.1
  25.0 3.5 %collective-permute-start.2 = (bf16[512,128]{1,0:T(8,128)(2,1)S(1)}, bf16[512,128]{1,0:T(8,128)(2,1)S(1)}, u32[]{:S(2)}, u32[]{:S(2)}) collective-permute-start(bf16[512,128]{1,0:T(8,128)(2,1)S(1)} %get-tuple-element.178), channel_id=1, source_target_pairs={{0,8},{8,16},{16,24},{24,32},{32,40},{40,48},{48,56},{56,64},{64,7... | collective-permute-start | bytes 393224 | tf_op jit(solution)/shard_map/while/body/eval_jaxpr/ppermute | solution.py:12
  32.2 4.1 %collective-permute-start = (s32[512]{0:T(512)S(1)}, s32[512]{0:T(512)S(1)}, u32[]{:S(2)}, u32[]{:S(2)}) collective-permute-start(s32[512]{0:T(512)S(1)} %get-tuple-element.179), channel_id=1, source_target_pairs={{0,8},{8,16},{16,24},{24,32},{32,40},{40,48},{48,56},{56,64},{64,7... | collective-permute-start | bytes 6152 | tf_op jit(solution)/shard_map/while/body/eval_jaxpr/ppermute | solution.py:12
  36.4 1.9 collective-permute-start.1
  38.3 3.2 %collective-permute-start.2 = (bf16[512,128]{1,0:T(8,128)(2,1)S(1)}, bf16[512,128]{1,0:T(8,128)(2,1)S(1)}, u32[]{:S(2)}, u32[]{:S(2)}) collective-permute-start(bf16[512,128]{1,0:T(8,128)(2,1)S(1)} %get-tuple-element.178), channel_id=1, source_target_pairs={{0,8},{8,16},{16,24},{24,32},{32,40},{40,48},{48,56},{56,64},{64,7... | collective-permute-start | bytes 393224 | tf_op jit(solution)/shard_map/while/body/eval_jaxpr/ppermute | solution.py:12
  43.6 1.5 fusion.56
  45.2 4.1 %collective-permute-start = (s32[512]{0:T(512)S(1)}, s32[512]{0:T(512)S(1)}, u32[]{:S(2)}, u32[]{:S(2)}) collective-permute-start(s32[512]{0:T(512)S(1)} %get-tuple-element.179), channel_id=1, source_target_pairs={{0,8},{8,16},{16,24},{24,32},{32,40},{40,48},{48,56},{56,64},{64,7... | collective-permute-start | bytes 6152 | tf_op jit(solution)/shard_map/while/body/eval_jaxpr/ppermute | solution.py:12
  49.3 1.9 collective-permute-start.1
  51.3 3.5 %collective-permute-start.2 = (bf16[512,128]{1,0:T(8,128)(2,1)S(1)}, bf16[512,128]{1,0:T(8,128)(2,1)S(1)}, u32[]{:S(2)}, u32[]{:S(2)}) collective-permute-start(bf16[512,128]{1,0:T(8,128)(2,1)S(1)} %get-tuple-element.178), channel_id=1, source_target_pairs={{0,8},{8,16},{16,24},{24,32},{32,40},{40,48},{48,56},{56,64},{64,7... | collective-permute-start | bytes 393224 | tf_op jit(solution)/shard_map/while/body/eval_jaxpr/ppermute | solution.py:12
  58.4 4.1 %collective-permute-start = (s32[512]{0:T(512)S(1)}, s32[512]{0:T(512)S(1)}, u32[]{:S(2)}, u32[]{:S(2)}) collective-permute-start(s32[512]{0:T(512)S(1)} %get-tuple-element.179), channel_id=1, source_target_pairs={{0,8},{8,16},{16,24},{24,32},{32,40},{40,48},{48,56},{56,64},{64,7... | collective-permute-start | bytes 6152 | tf_op jit(solution)/shard_map/while/body/eval_jaxpr/ppermute | solution.py:12
  62.6 3.4 %collective-permute-start.1 = (bf16[512,128]{1,0:T(8,128)(2,1)S(1)}, bf16[512,128]{1,0:T(8,128)(2,1)S(1)}, u32[]{:S(2)}, u32[]{:S(2)}) collective-permute-start(bf16[512,128]{1,0:T(8,128)(2,1)S(1)} %get-tuple-element.177), channel_id=1, source_target_pairs={{0,8},{8,16},{16,24},{24,32},{32,40},{40,48},{48,56},{56,64},{64,7... | collective-permute-start | bytes 393224 | tf_op jit(solution)/shard_map/while/body/eval_jaxpr/ppermute | solution.py:12
  66.0 4.1 %collective-permute-start.2 = (bf16[512,128]{1,0:T(8,128)(2,1)S(1)}, bf16[512,128]{1,0:T(8,128)(2,1)S(1)}, u32[]{:S(2)}, u32[]{:S(2)}) collective-permute-start(bf16[512,128]{1,0:T(8,128)(2,1)S(1)} %get-tuple-element.178), channel_id=1, source_target_pairs={{0,8},{8,16},{16,24},{24,32},{32,40},{40,48},{48,56},{56,64},{64,7... | collective-permute-start | bytes 393224 | tf_op jit(solution)/shard_map/while/body/eval_jaxpr/ppermute | solution.py:12
  73.8 4.1 %collective-permute-start = (s32[512]{0:T(512)S(1)}, s32[512]{0:T(512)S(1)}, u32[]{:S(2)}, u32[]{:S(2)}) collective-permute-start(s32[512]{0:T(512)S(1)} %get-tuple-element.179), channel_id=1, source_target_pairs={{0,8},{8,16},{16,24},{24,32},{32,40},{40,48},{48,56},{56,64},{64,7... | collective-permute-start | bytes 6152 | tf_op jit(solution)/shard_map/while/body/eval_jaxpr/ppermute | solution.py:12
  78.0 1.9 collective-permute-start.1
  79.9 4.0 %collective-permute-start.2 = (bf16[512,128]{1,0:T(8,128)(2,1)S(1)}, bf16[512,128]{1,0:T(8,128)(2,1)S(1)}, u32[]{:S(2)}, u32[]{:S(2)}) collective-permute-start(bf16[512,128]{1,0:T(8,128)(2,1)S(1)} %get-tuple-element.178), channel_id=1, source_target_pairs={{0,8},{8,16},{16,24},{24,32},{32,40},{40,48},{48,56},{56,64},{64,7... | collective-permute-start | bytes 393224 | tf_op jit(solution)/shard_map/while/body/eval_jaxpr/ppermute | solution.py:12
  87.6 4.1 %collective-permute-start = (s32[512]{0:T(512)S(1)}, s32[512]{0:T(512)S(1)}, u32[]{:S(2)}, u32[]{:S(2)}) collective-permute-start(s32[512]{0:T(512)S(1)} %get-tuple-element.179), channel_id=1, source_target_pairs={{0,8},{8,16},{16,24},{24,32},{32,40},{40,48},{48,56},{56,64},{64,7... | collective-permute-start | bytes 6152 | tf_op jit(solution)/shard_map/while/body/eval_jaxpr/ppermute | solution.py:12
  91.8 1.9 collective-permute-start.1
  93.7 4.0 %collective-permute-start.2 = (bf16[512,128]{1,0:T(8,128)(2,1)S(1)}, bf16[512,128]{1,0:T(8,128)(2,1)S(1)}, u32[]{:S(2)}, u32[]{:S(2)}) collective-permute-start(bf16[512,128]{1,0:T(8,128)(2,1)S(1)} %get-tuple-element.178), channel_id=1, source_target_pairs={{0,8},{8,16},{16,24},{24,32},{32,40},{40,48},{48,56},{56,64},{64,7... | collective-permute-start | bytes 393224 | tf_op jit(solution)/shard_map/while/body/eval_jaxpr/ppermute | solution.py:12
  99.9 1.5 fusion.56
  101.4 4.1 %collective-permute-start = (s32[512]{0:T(512)S(1)}, s32[512]{0:T(512)S(1)}, u32[]{:S(2)}, u32[]{:S(2)}) collective-permute-start(s32[512]{0:T(512)S(1)} %get-tuple-element.179), channel_id=1, source_target_pairs={{0,8},{8,16},{16,24},{24,32},{32,40},{40,48},{48,56},{56,64},{64,7... | collective-permute-start | bytes 6152 | tf_op jit(solution)/shard_map/while/body/eval_jaxpr/ppermute | solution.py:12
  105.6 1.9 collective-permute-start.1
  107.5 4.0 %collective-permute-start.2 = (bf16[512,128]{1,0:T(8,128)(2,1)S(1)}, bf16[512,128]{1,0:T(8,128)(2,1)S(1)}, u32[]{:S(2)}, u32[]{:S(2)}) collective-permute-start(bf16[512,128]{1,0:T(8,128)(2,1)S(1)} %get-tuple-element.178), channel_id=1, source_target_pairs={{0,8},{8,16},{16,24},{24,32},{32,40},{40,48},{48,56},{56,64},{64,7... | collective-permute-start | bytes 393224 | tf_op jit(solution)/shard_map/while/body/eval_jaxpr/ppermute | solution.py:12
  113.7 1.5 fusion.56
  115.2 4.1 %collective-permute-start = (s32[512]{0:T(512)S(1)}, s32[512]{0:T(512)S(1)}, u32[]{:S(2)}, u32[]{:S(2)}) collective-permute-start(s32[512]{0:T(512)S(1)} %get-tuple-element.179), channel_id=1, source_target_pairs={{0,8},{8,16},{16,24},{24,32},{32,40},{40,48},{48,56},{56,64},{64,7... | collective-permute-start | bytes 6152 | tf_op jit(solution)/shard_map/while/body/eval_jaxpr/ppermute | solution.py:12
  119.4 1.9 collective-permute-start.1
  121.3 4.0 %collective-permute-start.2 = (bf16[512,128]{1,0:T(8,128)(2,1)S(1)}, bf16[512,128]{1,0:T(8,128)(2,1)S(1)}, u32[]{:S(2)}, u32[]{:S(2)}) collective-permute-start(bf16[512,128]{1,0:T(8,128)(2,1)S(1)} %get-tuple-element.178), channel_id=1, source_target_pairs={{0,8},{8,16},{16,24},{24,32},{32,40},{40,48},{48,56},{56,64},{64,7... | collective-permute-start | bytes 393224 | tf_op jit(solution)/shard_map/while/body/eval_jaxpr/ppermute | solution.py:12
  130.3 59.2 %all-gather.2.cloned.1.call-done = bf16[512,4096]{0,1:T(8,128)(2,1)} async-done(((bf16[512,512]{0,1:T(8,128)(2,1)}), bf16[512,4096]{0,1:T(8,128)(2,1)}) %all-gather.2.cloned.1.call-update) | async-done | bytes 4194320 | tf_op jit(solution)/shard_map/all_gather | solution.py:83
  189.5 6.6 %convolution_convert_fusion = bf16[512,512]{1,0:T(8,128)(2,1)} fusion(bf16[512,4096]{0,1:T(8,128)(2,1)} %all-gather.2.cloned.1.call-done, bf16[4096,512]{1,0:T(8,128)(2,1)} %param.11), kind=kOutput, calls=%fused_computation.31 | convolution fusion | flops 2147745792 | bytes 8912896 | tf_op jit(solution)/shard_map/dot_general | solution.py:82
  (122 shorter events, 31.8 us)
Async XLA Ops:
  6.5 183.0 %all-gather.2.cloned.1.call-start = ((), (), s32[]{:S(2)}) async-start(), calls=%async_computation | async-start | bytes 4718592 | tf_op jit(solution)/shard_map/all_gather | solution.py:83
  12.8 1.9 copy-start
  18.6 10.0 %collective-permute-start = (s32[512]{0:T(512)S(1)}, s32[512]{0:T(512)S(1)}, u32[]{:S(2)}, u32[]{:S(2)}) collective-permute-start(s32[512]{0:T(512)S(1)} %get-tuple-element.179), channel_id=1, source_target_pairs={{0,8},{8,16},{16,24},{24,32},{32,40},{40,48},{48,56},{56,64},{64,7... | collective-permute-start | bytes 6152 | tf_op jit(solution)/shard_map/while/body/eval_jaxpr/ppermute | solution.py:12
  23.1 5.7 %collective-permute-start.1 = (bf16[512,128]{1,0:T(8,128)(2,1)S(1)}, bf16[512,128]{1,0:T(8,128)(2,1)S(1)}, u32[]{:S(2)}, u32[]{:S(2)}) collective-permute-start(bf16[512,128]{1,0:T(8,128)(2,1)S(1)} %get-tuple-element.177), channel_id=1, source_target_pairs={{0,8},{8,16},{16,24},{24,32},{32,40},{40,48},{48,56},{56,64},{64,7... | collective-permute-start | bytes 393224 | tf_op jit(solution)/shard_map/while/body/eval_jaxpr/ppermute | solution.py:12
  25.0 5.6 %collective-permute-start.2 = (bf16[512,128]{1,0:T(8,128)(2,1)S(1)}, bf16[512,128]{1,0:T(8,128)(2,1)S(1)}, u32[]{:S(2)}, u32[]{:S(2)}) collective-permute-start(bf16[512,128]{1,0:T(8,128)(2,1)S(1)} %get-tuple-element.178), channel_id=1, source_target_pairs={{0,8},{8,16},{16,24},{24,32},{32,40},{40,48},{48,56},{56,64},{64,7... | collective-permute-start | bytes 393224 | tf_op jit(solution)/shard_map/while/body/eval_jaxpr/ppermute | solution.py:12
  32.2 9.3 %collective-permute-start = (s32[512]{0:T(512)S(1)}, s32[512]{0:T(512)S(1)}, u32[]{:S(2)}, u32[]{:S(2)}) collective-permute-start(s32[512]{0:T(512)S(1)} %get-tuple-element.179), channel_id=1, source_target_pairs={{0,8},{8,16},{16,24},{24,32},{32,40},{40,48},{48,56},{56,64},{64,7... | collective-permute-start | bytes 6152 | tf_op jit(solution)/shard_map/while/body/eval_jaxpr/ppermute | solution.py:12
  36.4 5.4 %collective-permute-start.1 = (bf16[512,128]{1,0:T(8,128)(2,1)S(1)}, bf16[512,128]{1,0:T(8,128)(2,1)S(1)}, u32[]{:S(2)}, u32[]{:S(2)}) collective-permute-start(bf16[512,128]{1,0:T(8,128)(2,1)S(1)} %get-tuple-element.177), channel_id=1, source_target_pairs={{0,8},{8,16},{16,24},{24,32},{32,40},{40,48},{48,56},{56,64},{64,7... | collective-permute-start | bytes 393224 | tf_op jit(solution)/shard_map/while/body/eval_jaxpr/ppermute | solution.py:12
  38.3 5.3 %collective-permute-start.2 = (bf16[512,128]{1,0:T(8,128)(2,1)S(1)}, bf16[512,128]{1,0:T(8,128)(2,1)S(1)}, u32[]{:S(2)}, u32[]{:S(2)}) collective-permute-start(bf16[512,128]{1,0:T(8,128)(2,1)S(1)} %get-tuple-element.178), channel_id=1, source_target_pairs={{0,8},{8,16},{16,24},{24,32},{32,40},{40,48},{48,56},{56,64},{64,7... | collective-permute-start | bytes 393224 | tf_op jit(solution)/shard_map/while/body/eval_jaxpr/ppermute | solution.py:12
  45.2 9.6 %collective-permute-start = (s32[512]{0:T(512)S(1)}, s32[512]{0:T(512)S(1)}, u32[]{:S(2)}, u32[]{:S(2)}) collective-permute-start(s32[512]{0:T(512)S(1)} %get-tuple-element.179), channel_id=1, source_target_pairs={{0,8},{8,16},{16,24},{24,32},{32,40},{40,48},{48,56},{56,64},{64,7... | collective-permute-start | bytes 6152 | tf_op jit(solution)/shard_map/while/body/eval_jaxpr/ppermute | solution.py:12
  49.3 5.7 %collective-permute-start.1 = (bf16[512,128]{1,0:T(8,128)(2,1)S(1)}, bf16[512,128]{1,0:T(8,128)(2,1)S(1)}, u32[]{:S(2)}, u32[]{:S(2)}) collective-permute-start(bf16[512,128]{1,0:T(8,128)(2,1)S(1)} %get-tuple-element.177), channel_id=1, source_target_pairs={{0,8},{8,16},{16,24},{24,32},{32,40},{40,48},{48,56},{56,64},{64,7... | collective-permute-start | bytes 393224 | tf_op jit(solution)/shard_map/while/body/eval_jaxpr/ppermute | solution.py:12
  51.3 5.6 %collective-permute-start.2 = (bf16[512,128]{1,0:T(8,128)(2,1)S(1)}, bf16[512,128]{1,0:T(8,128)(2,1)S(1)}, u32[]{:S(2)}, u32[]{:S(2)}) collective-permute-start(bf16[512,128]{1,0:T(8,128)(2,1)S(1)} %get-tuple-element.178), channel_id=1, source_target_pairs={{0,8},{8,16},{16,24},{24,32},{32,40},{40,48},{48,56},{56,64},{64,7... | collective-permute-start | bytes 393224 | tf_op jit(solution)/shard_map/while/body/eval_jaxpr/ppermute | solution.py:12
  58.4 11.7 %collective-permute-start = (s32[512]{0:T(512)S(1)}, s32[512]{0:T(512)S(1)}, u32[]{:S(2)}, u32[]{:S(2)}) collective-permute-start(s32[512]{0:T(512)S(1)} %get-tuple-element.179), channel_id=1, source_target_pairs={{0,8},{8,16},{16,24},{24,32},{32,40},{40,48},{48,56},{56,64},{64,7... | collective-permute-start | bytes 6152 | tf_op jit(solution)/shard_map/while/body/eval_jaxpr/ppermute | solution.py:12
  62.6 7.8 %collective-permute-start.1 = (bf16[512,128]{1,0:T(8,128)(2,1)S(1)}, bf16[512,128]{1,0:T(8,128)(2,1)S(1)}, u32[]{:S(2)}, u32[]{:S(2)}) collective-permute-start(bf16[512,128]{1,0:T(8,128)(2,1)S(1)} %get-tuple-element.177), channel_id=1, source_target_pairs={{0,8},{8,16},{16,24},{24,32},{32,40},{40,48},{48,56},{56,64},{64,7... | collective-permute-start | bytes 393224 | tf_op jit(solution)/shard_map/while/body/eval_jaxpr/ppermute | solution.py:12
  66.0 6.3 %collective-permute-start.2 = (bf16[512,128]{1,0:T(8,128)(2,1)S(1)}, bf16[512,128]{1,0:T(8,128)(2,1)S(1)}, u32[]{:S(2)}, u32[]{:S(2)}) collective-permute-start(bf16[512,128]{1,0:T(8,128)(2,1)S(1)} %get-tuple-element.178), channel_id=1, source_target_pairs={{0,8},{8,16},{16,24},{24,32},{32,40},{40,48},{48,56},{56,64},{64,7... | collective-permute-start | bytes 393224 | tf_op jit(solution)/shard_map/while/body/eval_jaxpr/ppermute | solution.py:12
  73.8 10.1 %collective-permute-start = (s32[512]{0:T(512)S(1)}, s32[512]{0:T(512)S(1)}, u32[]{:S(2)}, u32[]{:S(2)}) collective-permute-start(s32[512]{0:T(512)S(1)} %get-tuple-element.179), channel_id=1, source_target_pairs={{0,8},{8,16},{16,24},{24,32},{32,40},{40,48},{48,56},{56,64},{64,7... | collective-permute-start | bytes 6152 | tf_op jit(solution)/shard_map/while/body/eval_jaxpr/ppermute | solution.py:12
  78.0 6.2 %collective-permute-start.1 = (bf16[512,128]{1,0:T(8,128)(2,1)S(1)}, bf16[512,128]{1,0:T(8,128)(2,1)S(1)}, u32[]{:S(2)}, u32[]{:S(2)}) collective-permute-start(bf16[512,128]{1,0:T(8,128)(2,1)S(1)} %get-tuple-element.177), channel_id=1, source_target_pairs={{0,8},{8,16},{16,24},{24,32},{32,40},{40,48},{48,56},{56,64},{64,7... | collective-permute-start | bytes 393224 | tf_op jit(solution)/shard_map/while/body/eval_jaxpr/ppermute | solution.py:12
  79.9 6.2 %collective-permute-start.2 = (bf16[512,128]{1,0:T(8,128)(2,1)S(1)}, bf16[512,128]{1,0:T(8,128)(2,1)S(1)}, u32[]{:S(2)}, u32[]{:S(2)}) collective-permute-start(bf16[512,128]{1,0:T(8,128)(2,1)S(1)} %get-tuple-element.178), channel_id=1, source_target_pairs={{0,8},{8,16},{16,24},{24,32},{32,40},{40,48},{48,56},{56,64},{64,7... | collective-permute-start | bytes 393224 | tf_op jit(solution)/shard_map/while/body/eval_jaxpr/ppermute | solution.py:12
  87.6 10.1 %collective-permute-start = (s32[512]{0:T(512)S(1)}, s32[512]{0:T(512)S(1)}, u32[]{:S(2)}, u32[]{:S(2)}) collective-permute-start(s32[512]{0:T(512)S(1)} %get-tuple-element.179), channel_id=1, source_target_pairs={{0,8},{8,16},{16,24},{24,32},{32,40},{40,48},{48,56},{56,64},{64,7... | collective-permute-start | bytes 6152 | tf_op jit(solution)/shard_map/while/body/eval_jaxpr/ppermute | solution.py:12
  91.8 6.2 %collective-permute-start.1 = (bf16[512,128]{1,0:T(8,128)(2,1)S(1)}, bf16[512,128]{1,0:T(8,128)(2,1)S(1)}, u32[]{:S(2)}, u32[]{:S(2)}) collective-permute-start(bf16[512,128]{1,0:T(8,128)(2,1)S(1)} %get-tuple-element.177), channel_id=1, source_target_pairs={{0,8},{8,16},{16,24},{24,32},{32,40},{40,48},{48,56},{56,64},{64,7... | collective-permute-start | bytes 393224 | tf_op jit(solution)/shard_map/while/body/eval_jaxpr/ppermute | solution.py:12
  93.7 6.2 %collective-permute-start.2 = (bf16[512,128]{1,0:T(8,128)(2,1)S(1)}, bf16[512,128]{1,0:T(8,128)(2,1)S(1)}, u32[]{:S(2)}, u32[]{:S(2)}) collective-permute-start(bf16[512,128]{1,0:T(8,128)(2,1)S(1)} %get-tuple-element.178), channel_id=1, source_target_pairs={{0,8},{8,16},{16,24},{24,32},{32,40},{40,48},{48,56},{56,64},{64,7... | collective-permute-start | bytes 393224 | tf_op jit(solution)/shard_map/while/body/eval_jaxpr/ppermute | solution.py:12
  101.4 10.1 %collective-permute-start = (s32[512]{0:T(512)S(1)}, s32[512]{0:T(512)S(1)}, u32[]{:S(2)}, u32[]{:S(2)}) collective-permute-start(s32[512]{0:T(512)S(1)} %get-tuple-element.179), channel_id=1, source_target_pairs={{0,8},{8,16},{16,24},{24,32},{32,40},{40,48},{48,56},{56,64},{64,7... | collective-permute-start | bytes 6152 | tf_op jit(solution)/shard_map/while/body/eval_jaxpr/ppermute | solution.py:12
  105.6 6.2 %collective-permute-start.1 = (bf16[512,128]{1,0:T(8,128)(2,1)S(1)}, bf16[512,128]{1,0:T(8,128)(2,1)S(1)}, u32[]{:S(2)}, u32[]{:S(2)}) collective-permute-start(bf16[512,128]{1,0:T(8,128)(2,1)S(1)} %get-tuple-element.177), channel_id=1, source_target_pairs={{0,8},{8,16},{16,24},{24,32},{32,40},{40,48},{48,56},{56,64},{64,7... | collective-permute-start | bytes 393224 | tf_op jit(solution)/shard_map/while/body/eval_jaxpr/ppermute | solution.py:12
  107.5 6.2 %collective-permute-start.2 = (bf16[512,128]{1,0:T(8,128)(2,1)S(1)}, bf16[512,128]{1,0:T(8,128)(2,1)S(1)}, u32[]{:S(2)}, u32[]{:S(2)}) collective-permute-start(bf16[512,128]{1,0:T(8,128)(2,1)S(1)} %get-tuple-element.178), channel_id=1, source_target_pairs={{0,8},{8,16},{16,24},{24,32},{32,40},{40,48},{48,56},{56,64},{64,7... | collective-permute-start | bytes 393224 | tf_op jit(solution)/shard_map/while/body/eval_jaxpr/ppermute | solution.py:12
  115.2 10.1 %collective-permute-start = (s32[512]{0:T(512)S(1)}, s32[512]{0:T(512)S(1)}, u32[]{:S(2)}, u32[]{:S(2)}) collective-permute-start(s32[512]{0:T(512)S(1)} %get-tuple-element.179), channel_id=1, source_target_pairs={{0,8},{8,16},{16,24},{24,32},{32,40},{40,48},{48,56},{56,64},{64,7... | collective-permute-start | bytes 6152 | tf_op jit(solution)/shard_map/while/body/eval_jaxpr/ppermute | solution.py:12
  119.4 6.2 %collective-permute-start.1 = (bf16[512,128]{1,0:T(8,128)(2,1)S(1)}, bf16[512,128]{1,0:T(8,128)(2,1)S(1)}, u32[]{:S(2)}, u32[]{:S(2)}) collective-permute-start(bf16[512,128]{1,0:T(8,128)(2,1)S(1)} %get-tuple-element.177), channel_id=1, source_target_pairs={{0,8},{8,16},{16,24},{24,32},{32,40},{40,48},{48,56},{56,64},{64,7... | collective-permute-start | bytes 393224 | tf_op jit(solution)/shard_map/while/body/eval_jaxpr/ppermute | solution.py:12
  121.3 6.2 %collective-permute-start.2 = (bf16[512,128]{1,0:T(8,128)(2,1)S(1)}, bf16[512,128]{1,0:T(8,128)(2,1)S(1)}, u32[]{:S(2)}, u32[]{:S(2)}) collective-permute-start(bf16[512,128]{1,0:T(8,128)(2,1)S(1)} %get-tuple-element.178), channel_id=1, source_target_pairs={{0,8},{8,16},{16,24},{24,32},{32,40},{40,48},{48,56},{56,64},{64,7... | collective-permute-start | bytes 393224 | tf_op jit(solution)/shard_map/while/body/eval_jaxpr/ppermute | solution.py:12
Sparse Core Ops, SparseCore 0:
  130.4 59.0 all-gather.1
where the time goes:
time: 204 us; the launch traced here: 203 us
  starting transfers between devices  80.8 us (40%)
  waiting for transfers between devices  59.3 us (29%)
  matrix products  31.2 us (15%)
  between operations  13.5 us (7%)
  other arithmetic  11.6 us (6%)
  local copies, waits for them, and re-layouts  5.57 us (3%)
    ppermute x24, starting transfers between devices, shifted(): return lax.ppermute(shard, axis, pairs)  80.8 us
    all_gather x1, waiting for transfers between devices, shards(): lax.all_gather(attended, 'head', axis=1, tiled=True)  59.2 us
    dot_general x9, matrix products, attend(): jnp.einsum('kgts,skd->kgtd', weights.astype(jnp.bfloat16), valued_rows, p...  15.6 us
    dot_general x9, matrix products, attend(): jnp.einsum('tkgd,skd->kgts', grouped_queries, keyed_rows, preferred_eleme...  8.97 us
    reduce_sum x9, other arithmetic, attend(): run_total = run_total * factor + jnp.sum(weights, axis=-1)  8.18 us
    dot_general x1, matrix products, shards(): jnp.dot(lax.all_gather(attended, 'head', axis=1, tiled=True), out_weight,...  6.61 us
  transfers between devices with their start and end apart: 25, of which 1 were waited for; matrix products, arithmetic and copies ran while one was open for 8% of the time, Pallas kernels for 0%

commit v1 on v0

v1 whole, which is shorter than its diff:
```python
import functools
import math

import jax
import jax.numpy as jnp
from jax import lax
from jax.experimental import pallas as pl
from jax.experimental.pallas import tpu as pltpu
from jax.sharding import PartitionSpec as P

HEAD_SIZE = 128
SCALE = HEAD_SIZE ** -0.5 * math.log2(math.e)
MASKED = -1e30
CHUNKS = 4
MESH = pl.DeviceIdType.MESH


def kernel(chips, planes, len_ref, q_hbm, k_hbm, v_hbm, w_hbm, o_ref,
           q, k_own, v_own, kb, vb, w, acc, top, first, att, gat, total,
           load_sem, kv_send, kv_recv, z_send, z_recv):
    tok = q.shape[0]
    feat = q.shape[1]
    heads = feat // HEAD_SIZE
    rows = tok // CHUNKS
    me = lax.axis_index("ctx")
    z = lax.axis_index("head")
    chip, core = me // 2, me % 2

    def peer(by):
        return {"ctx": lax.rem(chip + by + chips, chips) * 2 + core}

    sibling = {"ctx": chip * 2 + (1 - core)}
    right = {"head": lax.rem(z + 1, planes)}
    left = {"head": lax.rem(z + planes - 1, planes)}

    loads = [
        pltpu.make_async_copy(src, dst, load_sem.at[i])
        for i, (src, dst) in enumerate(((q_hbm, q), (k_hbm, k_own), (v_hbm, v_own), (w_hbm, w)))
    ]
    for c in (loads[1], loads[2], loads[0], loads[3]):
        c.start()

    barrier = pltpu.get_barrier_semaphore()
    sources = [peer(-j) for j in range(1, 5)] + [sibling, left, right]
    for d in sources:
        pl.semaphore_signal(barrier, inc=1, device_id=d, device_id_type=MESH)
    pl.semaphore_wait(barrier, len(sources))

    def kv_copies(src_k, src_v, slot, to):
        return [
            pltpu.make_async_remote_copy(
                src_ref=src, dst_ref=dst.at[slot], send_sem=kv_send.at[i, slot],
                recv_sem=kv_recv.at[i, slot], device_id=to, device_id_type=MESH)
            for i, (src, dst) in enumerate(((src_k, kb), (src_v, vb)))
        ]

    for j in (4, 3, 2, 1):
        for c in kv_copies(k_hbm, v_hbm, 2 * j - 2, peer(j)):
            c.start()
    for c in kv_copies(k_hbm, v_hbm, 8, sibling):
        c.start()

    lens = len_ref[...]
    docs = lens.shape[1]
    i0 = lax.broadcasted_iota(jnp.int32, (docs, docs), 0)
    i1 = lax.broadcasted_iota(jnp.int32, (docs, docs), 1)
    wide = jnp.broadcast_to(lens, (docs, docs))
    col = jnp.sum(jnp.where(i0 == i1, wide, 0), axis=1, keepdims=True)
    ends = jnp.sum(jnp.where(i0 <= i1, jnp.broadcast_to(col, (docs, docs)), 0), axis=0, keepdims=True)
    pos = me * tok + lax.broadcasted_iota(jnp.int32, (tok, docs), 0)
    ends = jnp.broadcast_to(ends, (tok, docs))
    began = jnp.max(jnp.where(ends <= pos, ends, 0), axis=1, keepdims=True)
    first[...] = jnp.broadcast_to(began, (tok, HEAD_SIZE))

    ones = jnp.ones((tok, HEAD_SIZE), jnp.bfloat16)
    spread = tok // HEAD_SIZE

    def attend(keys, vals, base, own):
        def one(h, carry):
            qh = q[:, pl.ds(pl.multiple_of(h * HEAD_SIZE, HEAD_SIZE), HEAD_SIZE)]
            s = lax.dot_general(qh, keys[...], (((1,), (1,)), ((), ())),
                                preferred_element_type=jnp.float32)
            at = lax.broadcasted_iota(jnp.int32, (tok, tok), 1)
            ok = at >= jnp.concatenate([first[...] - base] * spread, axis=1)
            if own:
                ok = ok & (at <= lax.broadcasted_iota(jnp.int32, (tok, tok), 0))
            s = jnp.where(ok, s, MASKED)
            new = jnp.broadcast_to(jnp.max(s, axis=1, keepdims=True), (tok, HEAD_SIZE))
            if not own:
                old = top[h]
                new = jnp.maximum(old, new)
            p = jnp.exp2((s - jnp.concatenate([new] * spread, axis=1)) * SCALE)
            both = jnp.dot(p.astype(jnp.bfloat16), jnp.concatenate([vals[...], ones], axis=1),
                           preferred_element_type=jnp.float32)
            if own:
                acc[h] = both
            else:
                fade = jnp.exp2((old - new) * SCALE)
                acc[h] = acc[h] * jnp.concatenate([fade, fade], axis=1) + both
            top[h] = new
            return carry

        lax.fori_loop(0, heads, one, 0)

    for c in loads[:3]:
        c.wait()
    attend(k_own, v_own, me * tok, True)

    for c in kv_copies(k_hbm, v_hbm, 8, sibling):
        c.wait_recv()

    def visit(n, carry):
        j, other = n // 2 + 1, n % 2
        for c in kv_copies(k_hbm, v_hbm, n, sibling):
            c.wait_recv()

        @pl.when(other == 0)
        def _():
            for c in kv_copies(kb.at[n], vb.at[n], n + 1, sibling):
                c.start()

        slot = jnp.where((n == 7) & (core == 1), 8, n)
        whose = jnp.where(other == 0, core, 1 - core)
        block = jnp.where(slot == 8, chip * 2, (chip - j) * 2 + whose)
        attend(kb.at[slot], vb.at[slot], block * tok, False)
        return carry

    lax.fori_loop(0, 8, visit, 0)

    def z_copy(src, t, slot, to):
        return pltpu.make_async_remote_copy(
            src_ref=src, dst_ref=gat.at[t, slot], send_sem=z_send.at[t, slot],
            recv_sem=z_recv.at[t, slot], device_id=to, device_id_type=MESH)

    last = planes - 2
    for t in range(CHUNKS):
        span = pl.ds(t * rows, rows)
        for h in range(heads):
            num = acc[h, span, 0:HEAD_SIZE]
            den = acc[h, span, HEAD_SIZE:2 * HEAD_SIZE]
            att[t, :, h * HEAD_SIZE:(h + 1) * HEAD_SIZE] = (num / den).astype(jnp.bfloat16)
        z_copy(att.at[t], t, 0, right).start()
        z_copy(att.at[t], t, last, left).start()

    def weight(by):
        plane = lax.rem(z + planes - by, planes)
        return w[pl.ds(pl.multiple_of(plane * feat, feat), feat), :]

    loads[3].wait()
    for t in range(CHUNKS):
        total[pl.ds(t * rows, rows), :] = jnp.dot(att[t], weight(0), preferred_element_type=jnp.float32)

    def add(t, slot):
        total[pl.ds(t * rows, rows), :] += jnp.dot(
            gat[t, slot], weight(slot + 1), preferred_element_type=jnp.float32)

    half = planes // 2
    for d in range(1, half + 1):
        for t in range(CHUNKS):
            far_right = half - t % 2
            far_left = planes - 1 - far_right
            if d <= far_right:
                z_copy(att.at[t], t, d - 1, right).wait_recv()
                if d < far_right:
                    z_copy(gat.at[t, d - 1], t, d, right).start()
            if d <= far_left:
                s = planes - 1 - d
                z_copy(att.at[t], t, s, left).wait_recv()
                if d < far_left:
                    z_copy(gat.at[t, s], t, s - 1, left).start()
            if d <= far_right:
                add(t, d - 1)
            if d <= far_left:
                add(t, planes - 1 - d)
    o_ref[...] = total[...].astype(o_ref.dtype)

    for slot in range(9):
        for c in kv_copies(k_hbm, v_hbm, slot, sibling):
            c.wait_send()
    for t in range(CHUNKS):
        for slot in range(planes - 1):
            z_copy(att.at[t], t, slot, right).wait_send()


def shards(chips, planes, queries, keys, values, lengths, out_weight):
    tok, feat = queries.shape
    heads = feat // HEAD_SIZE
    bf, f32 = jnp.bfloat16, jnp.float32
    rows = tok // CHUNKS
    hbm = pl.BlockSpec(memory_space=pl.ANY)
    return pl.pallas_call(
        functools.partial(kernel, chips, planes),
        out_shape=jax.ShapeDtypeStruct((tok, out_weight.shape[1]), bf),
        in_specs=[pl.BlockSpec(memory_space=pltpu.VMEM), hbm, hbm, hbm, hbm],
        out_specs=pl.BlockSpec(memory_space=pltpu.VMEM),
        scratch_shapes=[
            pltpu.VMEM((tok, feat), bf),
            pltpu.VMEM((tok, HEAD_SIZE), bf),
            pltpu.VMEM((tok, HEAD_SIZE), bf),
            pltpu.VMEM((9, tok, HEAD_SIZE), bf),
            pltpu.VMEM((9, tok, HEAD_SIZE), bf),
            pltpu.VMEM(out_weight.shape, bf),
            pltpu.VMEM((heads, tok, 2 * HEAD_SIZE), f32),
            pltpu.VMEM((heads, tok, HEAD_SIZE), f32),
            pltpu.VMEM((tok, HEAD_SIZE), jnp.int32),
            pltpu.VMEM((CHUNKS, rows, feat), bf),
            pltpu.VMEM((CHUNKS, planes - 1, rows, feat), bf),
            pltpu.VMEM((tok, out_weight.shape[1]), f32),
            pltpu.SemaphoreType.DMA((4,)),
            pltpu.SemaphoreType.DMA((2, 9)),
            pltpu.SemaphoreType.DMA((2, 9)),
            pltpu.SemaphoreType.DMA((CHUNKS, planes - 1)),
            pltpu.SemaphoreType.DMA((CHUNKS, planes - 1)),
        ],
        compiler_params=pltpu.CompilerParams(
            collective_id=0, has_side_effects=True, vmem_limit_bytes=62 * 2**20),
    )(lengths.reshape(1, -1), queries, keys, values, out_weight)


def solution(mesh):
    return jax.shard_map(
        functools.partial(shards, mesh.shape["ctx"] // 2, mesh.shape["head"]),
        mesh=mesh,
        in_specs=(P("ctx", "head"), P("ctx", "head"), P("ctx", "head"), P(), P(None, "head")),
        out_specs=P("ctx", "head"),
        check_vma=False,
    )
```

time: 204 us -> 99.5 us (0.49)
  Pallas kernels: 0 us -> 97.5 us
  starting transfers between devices: 80.8 us -> 0 us
  waiting for transfers between devices: 59.3 us -> 0 us
  matrix products: 31.2 us -> 0 us
  between operations: 13.5 us -> 0.01 us
  other arithmetic: 11.6 us -> 0 us
  local copies, waits for them, and re-layouts: 5.57 us -> 1.87 us
    pallas_call x0 -> x1, Pallas kernels: none -> 97.5 us  [shards(): pl.pallas_call(functools.partial(kernel, chips, planes), out_shape=jax.Sh...]
    ppermute x24 -> x0, starting transfers between devices: 80.8 us -> none  [shifted(): return lax.ppermute(shard, axis, pairs)]
    all_gather x1 -> x0, waiting for transfers between devices: 59.2 us -> none  [shards(): lax.all_gather(attended, 'head', axis=1, tiled=True)]
    dot_general x19 -> x0, matrix products: 31.2 us -> none  [the longest x9 15.6 us: attend(): jnp.einsum('kgts,skd->kgtd', weights.astype(jnp.bfloat16), valued_rows, p...]
    reduce_sum x10 -> x0, other arithmetic: 8.27 us -> none  [the longest x9 8.18 us: attend(): run_total = run_total * factor + jnp.sum(weights, axis=-1)]
    unnamed x6 -> x1, local copies, waits for them, and re-layouts: 4.02 us -> 1.87 us
  transfers between devices with their start and end apart: 25 -> 0, of which waited for: 1 -> 0; matrix products, arithmetic and copies ran while one was open for 8% -> 0% of each run, Pallas kernels for 0% -> 0%
where the time goes in v1:
time: 99.5 us; the launch traced here: 99.3 us
  Pallas kernels  97.5 us (98%)
  local copies, waits for them, and re-layouts  1.87 us (2%)
    pallas_call x1, Pallas kernels, shards(): pl.pallas_call(functools.partial(kernel, chips, planes), out_shape=jax.Sh...  97.5 us

profile of v1, /device:TPU:1, one launch (start us, length us, event | category | flops | bytes accessed | tf_op | source)
XLA Modules:
  0.0 99.3 jit_solution(17652343485923542395)
XLA Ops:
  0.0 97.5 %shard_map.55 = bf16[512,512]{1,0:T(8,128)(2,1)} custom-call(s32[1,64]{1,0:T(1,128)} %bitcast.1, bf16[512,512]{1,0:T(8,128)(2,1)} %q_hbm.1, bf16[512,128]{1,0:T(8,128)(2,1)} %k_hbm.1, bf16[512,128]{1,0:T(8,128)(2,1)} %v_hbm.1, bf16[4096,512]{1,0:T(8,128)(2,1)} %w_hbm.1), custom_call_target="tpu_custom_call" | custom-call | tf_op jit(solution)/shard_map/pallas_call | solution.py:191
  97.5 1.9 %copy.7 = bf16[512,512]{1,0:T(8,128)(2,1)} copy(bf16[512,512]{1,0:T(8,128)(2,1)} %shard_map.55) | data formatting | bytes 1048576

commit v2 on v1

--- a/solution.py
+++ b/solution.py
@@ -12,11 +12,14 @@
 SCALE = HEAD_SIZE ** -0.5 * math.log2(math.e)
 MASKED = -1e30
 CHUNKS = 4
+ROW = 4
+SAME = {2: 0, 3: 2, 1: 4, 4: 6}
+MATE = 8
 MESH = pl.DeviceIdType.MESH
 
 
 def kernel(chips, planes, len_ref, q_hbm, k_hbm, v_hbm, w_hbm, o_ref,
-           q, k_own, v_own, kb, vb, w, acc, top, first, att, gat, total,
+           q, k_own, v_own, kb, vb, w, acc, top, first, bias, tail, att, gat, total,
            load_sem, kv_send, kv_recv, z_send, z_recv):
     tok = q.shape[0]
     feat = q.shape[1]
@@ -25,10 +28,15 @@
     me = lax.axis_index("ctx")
     z = lax.axis_index("head")
     chip, core = me // 2, me % 2
-
-    def peer(by):
-        return {"ctx": lax.rem(chip + by + chips, chips) * 2 + core}
-
+    x = chip % ROW
+
+    def at_chip(c):
+        return {"ctx": c * 2 + core}
+
+    below = at_chip(lax.rem(chip + ROW, chips))
+    above = at_chip(lax.rem(chip + chips - ROW, chips))
+    east = at_chip(chip - x + lax.rem(x + 1, ROW))
+    west = at_chip(chip - x + lax.rem(x + ROW - 1, ROW))
     sibling = {"ctx": chip * 2 + (1 - core)}
     right = {"head": lax.rem(z + 1, planes)}
     left = {"head": lax.rem(z + planes - 1, planes)}
@@ -41,24 +49,38 @@
         c.start()
 
     barrier = pltpu.get_barrier_semaphore()
-    sources = [peer(-j) for j in range(1, 5)] + [sibling, left, right]
+    sources = [above, east, west, sibling, left, right]
     for d in sources:
         pl.semaphore_signal(barrier, inc=1, device_id=d, device_id_type=MESH)
     pl.semaphore_wait(barrier, len(sources))
 
-    def kv_copies(src_k, src_v, slot, to):
-        return [
-            pltpu.make_async_remote_copy(
-                src_ref=src, dst_ref=dst.at[slot], send_sem=kv_send.at[i, slot],
-                recv_sem=kv_recv.at[i, slot], device_id=to, device_id_type=MESH)
-            for i, (src, dst) in enumerate(((src_k, kb), (src_v, vb)))
-        ]
-
-    for j in (4, 3, 2, 1):
-        for c in kv_copies(k_hbm, v_hbm, 2 * j - 2, peer(j)):
-            c.start()
-    for c in kv_copies(k_hbm, v_hbm, 8, sibling):
-        c.start()
+    own = (k_hbm, v_hbm)
+    held = (kb, vb)
+
+    def send(i, src, slot, sem, to):
+        return pltpu.make_async_remote_copy(
+            src_ref=src, dst_ref=held[i].at[slot], send_sem=kv_send.at[i, sem],
+            recv_sem=kv_recv.at[i, slot], device_id=to, device_id_type=MESH)
+
+    def arrive(i, slot):
+        send(i, own[i], slot, 0, sibling).wait_recv()
+
+    def to_mate(i, j):
+        return send(i, held[i].at[SAME[j]], SAME[j] + 1, 5 + j, sibling)
+
+    for i in range(2):
+        send(i, own[i], SAME[4], 0, below).start()
+
+        @pl.when(x < ROW - 1)
+        def _():
+            send(i, own[i], SAME[1], 1, east).start()
+
+        @pl.when(x == 0)
+        def _():
+            send(i, own[i], SAME[3], 3, west).start()
+
+    for i in range(2):
+        send(i, own[i], MATE, 5, sibling).start()
 
     lens = len_ref[...]
     docs = lens.shape[1]
@@ -72,60 +94,117 @@
     began = jnp.max(jnp.where(ends <= pos, ends, 0), axis=1, keepdims=True)
     first[...] = jnp.broadcast_to(began, (tok, HEAD_SIZE))
 
-    ones = jnp.ones((tok, HEAD_SIZE), jnp.bfloat16)
     spread = tok // HEAD_SIZE
 
-    def attend(keys, vals, base, own):
-        def one(h, carry):
-            qh = q[:, pl.ds(pl.multiple_of(h * HEAD_SIZE, HEAD_SIZE), HEAD_SIZE)]
-            s = lax.dot_general(qh, keys[...], (((1,), (1,)), ((), ())),
-                                preferred_element_type=jnp.float32)
-            at = lax.broadcasted_iota(jnp.int32, (tok, tok), 1)
-            ok = at >= jnp.concatenate([first[...] - base] * spread, axis=1)
-            if own:
-                ok = ok & (at <= lax.broadcasted_iota(jnp.int32, (tok, tok), 0))
-            s = jnp.where(ok, s, MASKED)
-            new = jnp.broadcast_to(jnp.max(s, axis=1, keepdims=True), (tok, HEAD_SIZE))
-            if not own:
-                old = top[h]
+    def limits(r0, m, bases, causal):
+        parts = []
+        lane = lax.broadcasted_iota(jnp.int32, (m, tok), 1)
+        for base in bases:
+            ok = lane >= jnp.concatenate([first[r0:r0 + m, :] - base] * spread, axis=1)
+            if causal:
+                ok = ok & (lane <= lax.broadcasted_iota(jnp.int32, (m, tok), 0))
+            parts.append(jnp.where(ok, jnp.float32(-MASKED), jnp.float32(MASKED)))
+        return parts[0] if len(parts) == 1 else jnp.concatenate(parts, axis=1)
+
+    def attend(r0, m, keys, vals, limit, fresh):
+        wide = keys.shape[0]
+        vals = jnp.concatenate([vals, jnp.ones((wide, HEAD_SIZE), jnp.bfloat16)], axis=1)
+        span = slice(r0, r0 + m)
+
+        def score(h):
+            return lax.dot_general(q[span, h * HEAD_SIZE:(h + 1) * HEAD_SIZE], keys, (((1,), (1,)), ((), ())),
+                                   preferred_element_type=jnp.float32)
+
+        ahead = score(0)
+        for h in range(heads):
+            s = ahead
+            if h + 1 < heads:
+                ahead = score(h + 1)
+            s = jnp.minimum(s, limit[...])
+            new = jnp.broadcast_to(jnp.max(s, axis=1, keepdims=True), (m, HEAD_SIZE))
+            if not fresh:
+                old = top[h, span, :]
                 new = jnp.maximum(old, new)
-            p = jnp.exp2((s - jnp.concatenate([new] * spread, axis=1)) * SCALE)
-            both = jnp.dot(p.astype(jnp.bfloat16), jnp.concatenate([vals[...], ones], axis=1),
-                           preferred_element_type=jnp.float32)
-            if own:
-                acc[h] = both
+            p = jnp.exp2((s - jnp.concatenate([new] * (wide // HEAD_SIZE), axis=1)) * SCALE)
+            both = jnp.dot(p.astype(jnp.bfloat16), vals, preferred_element_type=jnp.float32)
+            if fresh:
+                acc[h, span, :] = both
             else:
                 fade = jnp.exp2((old - new) * SCALE)
-                acc[h] = acc[h] * jnp.concatenate([fade, fade], axis=1) + both
-            top[h] = new
-            return carry
-
-        lax.fori_loop(0, heads, one, 0)
+                acc[h, span, :] = acc[h, span, :] * jnp.concatenate([fade, fade], axis=1) + both
+            top[h, span, :] = new
 
     for c in loads[:3]:
         c.wait()
-    attend(k_own, v_own, me * tok, True)
-
-    for c in kv_copies(k_hbm, v_hbm, 8, sibling):
-        c.wait_recv()
-
-    def visit(n, carry):
-        j, other = n // 2 + 1, n % 2
-        for c in kv_copies(k_hbm, v_hbm, n, sibling):
-            c.wait_recv()
-
-        @pl.when(other == 0)
-        def _():
-            for c in kv_copies(kb.at[n], vb.at[n], n + 1, sibling):
-                c.start()
-
-        slot = jnp.where((n == 7) & (core == 1), 8, n)
-        whose = jnp.where(other == 0, core, 1 - core)
-        block = jnp.where(slot == 8, chip * 2, (chip - j) * 2 + whose)
-        attend(kb.at[slot], vb.at[slot], block * tok, False)
+    bias[...] = limits(0, tok, [me * tok], True)
+    attend(0, tok, k_own[...], v_own[...], bias, True)
+
+    for i in range(2):
+        arrive(i, SAME[4])
+
+        @pl.when(x == ROW - 1)
+        def _():
+            send(i, held[i].at[SAME[4]], SAME[1], 1, east).start()
+
+        @pl.when(x > 0)
+        def _():
+            send(i, held[i].at[SAME[4]], SAME[3], 3, west).start()
+
+        to_mate(i, 4).start()
+    for i in range(2):
+        arrive(i, SAME[1])
+
+        @pl.when((x < ROW - 1) if i == 0 else (x == ROW - 2))
+        def _():
+            send(i, held[i].at[SAME[1]], SAME[2], 2, east).start()
+
+        to_mate(i, 1).start()
+
+    def from_row(i):
+        arrive(i, SAME[3])
+
+        @pl.when((x == 1) if i == 0 else (x > 0))
+        def _():
+            send(i, held[i].at[SAME[3]], SAME[2], 4, west).start()
+
+        to_mate(i, 3).start()
+
+    from_row(0)
+    for i in range(2):
+        arrive(i, MATE)
+        arrive(i, SAME[4] + 1)
+
+    def far(n, carry):
+        mine = jnp.where(core == 1, MATE, SAME[4] + 1)
+        slot = jnp.where(n == 0, SAME[4], mine)
+        block = jnp.where(n == 0, (chip - 4) * 2 + core, jnp.where(core == 1, chip * 2, (chip - 4) * 2 + 1))
+        bias[...] = limits(0, tok, [block * tok], False)
+        attend(0, tok, kb[slot], vb[slot], bias, False)
         return carry
 
-    lax.fori_loop(0, 8, visit, 0)
+    lax.fori_loop(0, 2, far, 0)
+    from_row(1)
+    for i in range(2):
+        arrive(i, SAME[1] + 1)
+
+    def near(n, carry):
+        block = (chip - 1) * 2 + jnp.where(n == 0, core, 1 - core)
+        bias[...] = limits(0, tok, [block * tok], False)
+        attend(0, tok, kb[SAME[1] + n], vb[SAME[1] + n], bias, False)
+        arrive_mid(n)
+        return carry
+
+    def arrive_mid(n):
+        for i in range(2):
+            @pl.when(n == i)
+            def _():
+                arrive(i, SAME[2])
+                to_mate(i, 2).start()
+
+    lax.fori_loop(0, 2, near, 0)
+    for i in range(2):
+        arrive(i, SAME[3] + 1)
+        arrive(i, SAME[2] + 1)
 
     def z_copy(src, t, slot, to):
         return pltpu.make_async_remote_copy(
@@ -133,7 +212,12 @@
             recv_sem=z_recv.at[t, slot], device_id=to, device_id_type=MESH)
 
     last = planes - 2
+    bases = [((chip - j) * 2 + c) * tok for j in (2, 3) for c in (core, 1 - core)]
+    late = len(bases)
     for t in range(CHUNKS):
+        tail[...] = limits(t * rows, rows, bases, False)
+        attend(t * rows, rows, kb[0:late].reshape(late * tok, HEAD_SIZE), vb[0:late].reshape(late * tok, HEAD_SIZE),
+               tail, False)
         span = pl.ds(t * rows, rows)
         for h in range(heads):
             num = acc[h, span, 0:HEAD_SIZE]
@@ -174,9 +258,21 @@
                 add(t, planes - 1 - d)
     o_ref[...] = total[...].astype(o_ref.dtype)
 
-    for slot in range(9):
-        for c in kv_copies(k_hbm, v_hbm, slot, sibling):
-            c.wait_send()
+    def sent(i, sem):
+        send(i, own[i], MATE, sem, sibling).wait_send()
+
+    for i in range(2):
+        for sem in (0, 1, 3, 5, 6, 7, 8, 9):
+            sent(i, sem)
+
+        @pl.when((x < ROW - 1) if i == 0 else (x == ROW - 2))
+        def _():
+            sent(i, 2)
+
+        @pl.when((x == 1) if i == 0 else (x > 0))
+        def _():
+            sent(i, 4)
+
     for t in range(CHUNKS):
         for slot in range(planes - 1):
             z_copy(att.at[t], t, slot, right).wait_send()
@@ -203,11 +299,13 @@
             pltpu.VMEM((heads, tok, 2 * HEAD_SIZE), f32),
             pltpu.VMEM((heads, tok, HEAD_SIZE), f32),
             pltpu.VMEM((tok, HEAD_SIZE), jnp.int32),
+            pltpu.VMEM((tok, tok), f32),
+            pltpu.VMEM((rows, 4 * tok), f32),
             pltpu.VMEM((CHUNKS, rows, feat), bf),
             pltpu.VMEM((CHUNKS, planes - 1, rows, feat), bf),
             pltpu.VMEM((tok, out_weight.shape[1]), f32),
             pltpu.SemaphoreType.DMA((4,)),
-            pltpu.SemaphoreType.DMA((2, 9)),
+            pltpu.SemaphoreType.DMA((2, 10)),
             pltpu.SemaphoreType.DMA((2, 9)),
             pltpu.SemaphoreType.DMA((CHUNKS, planes - 1)),
             pltpu.SemaphoreType.DMA((CHUNKS, planes - 1)),

time: 99.5 us -> 77.5 us (0.78)
  Pallas kernels: 97.5 us -> 75.4 us
    pallas_call x1, Pallas kernels: 97.5 us -> 75.4 us  [shards(): pl.pallas_call(functools.partial(kernel, chips, planes), out_shape=jax.Sh...]
where the time goes in v2:
time: 77.5 us; the launch traced here: 77.3 us
  Pallas kernels  75.4 us (97%)
  local copies, waits for them, and re-layouts  1.87 us (2%)
    pallas_call x1, Pallas kernels, shards(): pl.pallas_call(functools.partial(kernel, chips, planes), out_shape=jax.Sh...  75.4 us
    unnamed x1, local copies, waits for them, and re-layouts  1.87 us

profile of v2, /device:TPU:1, one launch (start us, length us, event | category | flops | bytes accessed | tf_op | source)
XLA Modules:
  0.0 77.3 jit_solution(8202360033059963360)
XLA Ops:
  0.0 75.4 %shard_map.55 = bf16[512,512]{1,0:T(8,128)(2,1)} custom-call(s32[1,64]{1,0:T(1,128)} %bitcast.1, bf16[512,512]{1,0:T(8,128)(2,1)} %q_hbm.1, bf16[512,128]{1,0:T(8,128)(2,1)} %k_hbm.1, bf16[512,128]{1,0:T(8,128)(2,1)} %v_hbm.1, bf16[4096,512]{1,0:T(8,128)(2,1)} %w_hbm.1), custom_call_target="tpu_custom_call" | custom-call | tf_op jit(solution)/shard_map/pallas_call | solution.py:287
  75.5 1.9 %copy.7 = bf16[512,512]{1,0:T(8,128)(2,1)} copy(bf16[512,512]{1,0:T(8,128)(2,1)} %shard_map.55) | data formatting | bytes 1048576

commit v3 on v2

--- a/solution.py
+++ b/solution.py
@@ -13,14 +13,15 @@
 MASKED = -1e30
 CHUNKS = 4
 ROW = 4
+PIECES = 2
 SAME = {2: 0, 3: 2, 1: 4, 4: 6}
 MATE = 8
 MESH = pl.DeviceIdType.MESH
 
 
 def kernel(chips, planes, len_ref, q_hbm, k_hbm, v_hbm, w_hbm, o_ref,
-           q, k_own, v_own, kb, vb, w, acc, top, first, bias, tail, att, gat, total,
-           load_sem, kv_send, kv_recv, z_send, z_recv):
+           q, k_own, v_own, kb, vb, w, acc, top, first, bias, tail, att, gat, total, out,
+           load_sem, kv_send, kv_recv, z_send, z_recv, out_sem):
     tok = q.shape[0]
     feat = q.shape[1]
     heads = feat // HEAD_SIZE
@@ -35,8 +36,9 @@
 
     below = at_chip(lax.rem(chip + ROW, chips))
     above = at_chip(lax.rem(chip + chips - ROW, chips))
-    east = at_chip(chip - x + lax.rem(x + 1, ROW))
-    west = at_chip(chip - x + lax.rem(x + ROW - 1, ROW))
+    peers = [at_chip(chip - x + lax.rem(x + j, ROW)) for j in range(1, ROW)]
+    ahead_two = at_chip(lax.rem(chip + 2, chips))
+    behind_two = at_chip(lax.rem(chip + chips - 2, chips))
     sibling = {"ctx": chip * 2 + (1 - core)}
     right = {"head": lax.rem(z + 1, planes)}
     left = {"head": lax.rem(z + planes - 1, planes)}
@@ -49,38 +51,51 @@
         c.start()
 
     barrier = pltpu.get_barrier_semaphore()
-    sources = [above, east, west, sibling, left, right]
+    sources = [above, *peers, behind_two, sibling, left, right]
     for d in sources:
         pl.semaphore_signal(barrier, inc=1, device_id=d, device_id_type=MESH)
     pl.semaphore_wait(barrier, len(sources))
 
-    own = (k_hbm, v_hbm)
-    held = (kb, vb)
+    part = tok // PIECES
+    pieces = range(2 * PIECES)
+
+    def piece(refs, i, *at):
+        return refs[i // PIECES].at[(*at, pl.ds(i % PIECES * part, part))]
 
     def send(i, src, slot, sem, to):
         return pltpu.make_async_remote_copy(
-            src_ref=src, dst_ref=held[i].at[slot], send_sem=kv_send.at[i, sem],
+            src_ref=src, dst_ref=piece((kb, vb), i, slot), send_sem=kv_send.at[i, sem],
             recv_sem=kv_recv.at[i, slot], device_id=to, device_id_type=MESH)
 
+    def own(i):
+        return piece((k_hbm, v_hbm), i)
+
     def arrive(i, slot):
-        send(i, own[i], slot, 0, sibling).wait_recv()
-
-    def to_mate(i, j):
-        return send(i, held[i].at[SAME[j]], SAME[j] + 1, 5 + j, sibling)
-
-    for i in range(2):
-        send(i, own[i], SAME[4], 0, below).start()
-
-        @pl.when(x < ROW - 1)
-        def _():
-            send(i, own[i], SAME[1], 1, east).start()
-
-        @pl.when(x == 0)
-        def _():
-            send(i, own[i], SAME[3], 3, west).start()
-
-    for i in range(2):
-        send(i, own[i], MATE, 5, sibling).start()
+        send(i, own(i), slot, 0, sibling).wait_recv()
+
+    def from_chip(i, j):
+        arrive(i, SAME[j])
+        send(i, piece((kb, vb), i, SAME[j]), SAME[j] + 1, 5 + j, sibling).start()
+
+    for i in pieces:
+        send(i, own(i), SAME[4], 0, below).start()
+        for j in (1, 3, 2):
+            @pl.when(x + j < ROW)
+            def _():
+                send(i, own(i), SAME[j], j, peers[j - 1]).start()
+
+    @pl.when(x == ROW - 2)
+    def _():
+        for i in pieces:
+            send(i, own(i), SAME[2], 2, ahead_two).start()
+
+    @pl.when(x == ROW - 1)
+    def _():
+        for i in pieces[PIECES:]:
+            send(i, own(i), SAME[2], 2, ahead_two).start()
+
+    for i in pieces:
+        send(i, own(i), MATE, 5, sibling).start()
 
     lens = len_ref[...]
     docs = lens.shape[1]
@@ -139,38 +154,15 @@
     bias[...] = limits(0, tok, [me * tok], True)
     attend(0, tok, k_own[...], v_own[...], bias, True)
 
-    for i in range(2):
+    for i in pieces:
         arrive(i, SAME[4])
-
-        @pl.when(x == ROW - 1)
-        def _():
-            send(i, held[i].at[SAME[4]], SAME[1], 1, east).start()
-
-        @pl.when(x > 0)
-        def _():
-            send(i, held[i].at[SAME[4]], SAME[3], 3, west).start()
-
-        to_mate(i, 4).start()
-    for i in range(2):
-        arrive(i, SAME[1])
-
-        @pl.when((x < ROW - 1) if i == 0 else (x == ROW - 2))
-        def _():
-            send(i, held[i].at[SAME[1]], SAME[2], 2, east).start()
-
-        to_mate(i, 1).start()
-
-    def from_row(i):
-        arrive(i, SAME[3])
-
-        @pl.when((x == 1) if i == 0 else (x > 0))
-        def _():
-            send(i, held[i].at[SAME[3]], SAME[2], 4, west).start()
-
-        to_mate(i, 3).start()
-
-    from_row(0)
-    for i in range(2):
+        for j in (3, 1, 2)[:3 if i < PIECES else 2]:
+            @pl.when((x + j >= ROW) if j != 2 else (x == ROW - 1))
+            def _():
+                send(i, piece((kb, vb), i, SAME[4]), SAME[j], j, peers[j - 1]).start()
+    for i in pieces:
+        send(i, piece((kb, vb), i, SAME[4]), SAME[4] + 1, 9, sibling).start()
+    for i in pieces:
         arrive(i, MATE)
         arrive(i, SAME[4] + 1)
 
@@ -183,28 +175,9 @@
         return carry
 
     lax.fori_loop(0, 2, far, 0)
-    from_row(1)
-    for i in range(2):
-        arrive(i, SAME[1] + 1)
-
-    def near(n, carry):
-        block = (chip - 1) * 2 + jnp.where(n == 0, core, 1 - core)
-        bias[...] = limits(0, tok, [block * tok], False)
-        attend(0, tok, kb[SAME[1] + n], vb[SAME[1] + n], bias, False)
-        arrive_mid(n)
-        return carry
-
-    def arrive_mid(n):
-        for i in range(2):
-            @pl.when(n == i)
-            def _():
-                arrive(i, SAME[2])
-                to_mate(i, 2).start()
-
-    lax.fori_loop(0, 2, near, 0)
-    for i in range(2):
-        arrive(i, SAME[3] + 1)
-        arrive(i, SAME[2] + 1)
+    for j in (1, 3, 2):
+        for i in pieces:
+            from_chip(i, j)
 
     def z_copy(src, t, slot, to):
         return pltpu.make_async_remote_copy(
@@ -212,12 +185,25 @@
             recv_sem=z_recv.at[t, slot], device_id=to, device_id_type=MESH)
 
     last = planes - 2
-    bases = [((chip - j) * 2 + c) * tok for j in (2, 3) for c in (core, 1 - core)]
-    late = len(bases)
+    bases = [((chip - j) * 2 + c) * tok for j in (2, 3, 1) for c in (core, 1 - core)]
+
+    def attend_slots(t, low, high):
+        wide = (high - low) * tok
+        limit = tail.at[:, low * tok:high * tok]
+        limit[...] = limits(t * rows, rows, bases[low:high], False)
+        attend(t * rows, rows, kb[low:high].reshape(wide, HEAD_SIZE), vb[low:high].reshape(wide, HEAD_SIZE), limit, False)
+
     for t in range(CHUNKS):
-        tail[...] = limits(t * rows, rows, bases, False)
-        attend(t * rows, rows, kb[0:late].reshape(late * tok, HEAD_SIZE), vb[0:late].reshape(late * tok, HEAD_SIZE),
-               tail, False)
+        if t == 0:
+            for i in pieces:
+                arrive(i, SAME[1] + 1)
+            attend_slots(t, 4, 6)
+            for i in pieces:
+                arrive(i, SAME[3] + 1)
+                arrive(i, SAME[2] + 1)
+            attend_slots(t, 0, 4)
+        else:
+            attend_slots(t, 0, 6)
         span = pl.ds(t * rows, rows)
         for h in range(heads):
             num = acc[h, span, 0:HEAD_SIZE]
@@ -237,6 +223,10 @@
     def add(t, slot):
         total[pl.ds(t * rows, rows), :] += jnp.dot(
             gat[t, slot], weight(slot + 1), preferred_element_type=jnp.float32)
+
+    def out_copy(t):
+        span = pl.ds(t * rows, rows)
+        return pltpu.make_async_copy(out.at[span], o_ref.at[span], out_sem.at[t])
 
     half = planes // 2
     for d in range(1, half + 1):
@@ -256,23 +246,16 @@
                 add(t, d - 1)
             if d <= far_left:
                 add(t, planes - 1 - d)
-    o_ref[...] = total[...].astype(o_ref.dtype)
-
-    def sent(i, sem):
-        send(i, own[i], MATE, sem, sibling).wait_send()
-
-    for i in range(2):
-        for sem in (0, 1, 3, 5, 6, 7, 8, 9):
-            sent(i, sem)
-
-        @pl.when((x < ROW - 1) if i == 0 else (x == ROW - 2))
-        def _():
-            sent(i, 2)
-
-        @pl.when((x == 1) if i == 0 else (x > 0))
-        def _():
-            sent(i, 4)
-
+            if d == half:
+                span = pl.ds(t * rows, rows)
+                out[span, :] = total[span, :].astype(out.dtype)
+                out_copy(t).start()
+    for t in range(CHUNKS):
+        out_copy(t).wait()
+
+    for i in pieces:
+        for sem in (0, 1, 2, 3, 5, 6, 7, 8, 9):
+            send(i, own(i), MATE, sem, sibling).wait_send()
     for t in range(CHUNKS):
         for slot in range(planes - 1):
             z_copy(att.at[t], t, slot, right).wait_send()
@@ -288,7 +271,7 @@
         functools.partial(kernel, chips, planes),
         out_shape=jax.ShapeDtypeStruct((tok, out_weight.shape[1]), bf),
         in_specs=[pl.BlockSpec(memory_space=pltpu.VMEM), hbm, hbm, hbm, hbm],
-        out_specs=pl.BlockSpec(memory_space=pltpu.VMEM),
+        out_specs=hbm,
         scratch_shapes=[
             pltpu.VMEM((tok, feat), bf),
             pltpu.VMEM((tok, HEAD_SIZE), bf),
@@ -300,15 +283,17 @@
             pltpu.VMEM((heads, tok, HEAD_SIZE), f32),
             pltpu.VMEM((tok, HEAD_SIZE), jnp.int32),
             pltpu.VMEM((tok, tok), f32),
-            pltpu.VMEM((rows, 4 * tok), f32),
+            pltpu.VMEM((rows, 6 * tok), f32),
             pltpu.VMEM((CHUNKS, rows, feat), bf),
             pltpu.VMEM((CHUNKS, planes - 1, rows, feat), bf),
             pltpu.VMEM((tok, out_weight.shape[1]), f32),
+            pltpu.VMEM((tok, out_weight.shape[1]), bf),
             pltpu.SemaphoreType.DMA((4,)),
-            pltpu.SemaphoreType.DMA((2, 10)),
-            pltpu.SemaphoreType.DMA((2, 9)),
+            pltpu.SemaphoreType.DMA((2 * PIECES, 10)),
+            pltpu.SemaphoreType.DMA((2 * PIECES, 9)),
             pltpu.SemaphoreType.DMA((CHUNKS, planes - 1)),
             pltpu.SemaphoreType.DMA((CHUNKS, planes - 1)),
+            pltpu.SemaphoreType.DMA((CHUNKS,)),
         ],
         compiler_params=pltpu.CompilerParams(
             collective_id=0, has_side_effects=True, vmem_limit_bytes=62 * 2**20),

time: 77.5 us -> 76.1 us (0.982)
  Pallas kernels: 75.4 us -> 74.1 us
    pallas_call x1, Pallas kernels: 75.4 us -> 74.1 us  [shards(): pl.pallas_call(functools.partial(kernel, chips, planes), out_shape=jax.Sh...]
where the time goes in v3:
time: 76.1 us; the launch traced here: 75.9 us
  Pallas kernels  74.1 us (97%)
  local copies, waits for them, and re-layouts  1.87 us (2%)
    pallas_call x1, Pallas kernels, shards(): pl.pallas_call(functools.partial(kernel, chips, planes), out_shape=jax.Sh...  74.1 us
    unnamed x1, local copies, waits for them, and re-layouts  1.87 us

profile of v3, /device:TPU:1, one launch (start us, length us, event | category | flops | bytes accessed | tf_op | source)
XLA Modules:
  0.0 75.9 jit_solution(12843647705630098088)
XLA Ops:
  0.0 74.1 %shard_map.55 = bf16[512,512]{1,0:T(8,128)(2,1)} custom-call(s32[1,64]{1,0:T(1,128)} %bitcast.1, bf16[512,512]{1,0:T(8,128)(2,1)} %q_hbm.1, bf16[512,128]{1,0:T(8,128)(2,1)} %k_hbm.1, bf16[512,128]{1,0:T(8,128)(2,1)} %v_hbm.1, bf16[4096,512]{1,0:T(8,128)(2,1)} %w_hbm.1), custom_call_target="tpu_custom_call" | custom-call | tf_op jit(solution)/shard_map/pallas_call | solution.py:270
  74.1 1.9 %copy.7 = bf16[512,512]{1,0:T(8,128)(2,1)} copy(bf16[512,512]{1,0:T(8,128)(2,1)} %shard_map.55) | data formatting | bytes 1048576

commit v4 on v3

--- a/solution.py
+++ b/solution.py
@@ -47,7 +47,7 @@
         pltpu.make_async_copy(src, dst, load_sem.at[i])
         for i, (src, dst) in enumerate(((q_hbm, q), (k_hbm, k_own), (v_hbm, v_own), (w_hbm, w)))
     ]
-    for c in (loads[1], loads[2], loads[0], loads[3]):
+    for c in (loads[1], loads[2], loads[0]):
         c.start()
 
     barrier = pltpu.get_barrier_semaphore()
@@ -96,6 +96,8 @@
 
     for i in pieces:
         send(i, own(i), MATE, 5, sibling).start()
+
+    loads[3].start()
 
     lens = len_ref[...]
     docs = lens.shape[1]
@@ -156,7 +158,7 @@
 
     for i in pieces:
         arrive(i, SAME[4])
-        for j in (3, 1, 2)[:3 if i < PIECES else 2]:
+        for j in (1, 3, 2)[:3 if i < PIECES else 2]:
             @pl.when((x + j >= ROW) if j != 2 else (x == ROW - 1))
             def _():
                 send(i, piece((kb, vb), i, SAME[4]), SAME[j], j, peers[j - 1]).start()

time: 76.1 us -> 76.1 us (level)
  no operation moved by 1% of the time
where the time goes in v4:
time: 76.1 us; the launch traced here: 76 us
  Pallas kernels  74.1 us (97%)
  local copies, waits for them, and re-layouts  1.87 us (2%)
    pallas_call x1, Pallas kernels, shards(): pl.pallas_call(functools.partial(kernel, chips, planes), out_shape=jax.Sh...  74.1 us
    unnamed x1, local copies, waits for them, and re-layouts  1.87 us

profile of v4, /device:TPU:1, one launch (start us, length us, event | category | flops | bytes accessed | tf_op | source)
XLA Modules:
  0.0 76.0 jit_solution(17318528060387579672)
XLA Ops:
  0.0 74.1 %shard_map.55 = bf16[512,512]{1,0:T(8,128)(2,1)} custom-call(s32[1,64]{1,0:T(1,128)} %bitcast.1, bf16[512,512]{1,0:T(8,128)(2,1)} %q_hbm.1, bf16[512,128]{1,0:T(8,128)(2,1)} %k_hbm.1, bf16[512,128]{1,0:T(8,128)(2,1)} %v_hbm.1, bf16[4096,512]{1,0:T(8,128)(2,1)} %w_hbm.1), custom_call_target="tpu_custom_call" | custom-call | tf_op jit(solution)/shard_map/pallas_call | solution.py:272
  74.1 1.9 %copy.7 = bf16[512,512]{1,0:T(8,128)(2,1)} copy(bf16[512,512]{1,0:T(8,128)(2,1)} %shard_map.55) | data formatting | bytes 1048576

commit v5 on v4

--- a/solution.py
+++ b/solution.py
@@ -177,7 +177,7 @@
         return carry
 
     lax.fori_loop(0, 2, far, 0)
-    for j in (1, 3, 2):
+    for j in (2, 1):
         for i in pieces:
             from_chip(i, j)
 
@@ -198,12 +198,17 @@
     for t in range(CHUNKS):
         if t == 0:
             for i in pieces:
+                arrive(i, SAME[2] + 1)
+            attend_slots(t, 0, 2)
+            for i in pieces:
+                from_chip(i, 3)
+            for i in pieces:
                 arrive(i, SAME[1] + 1)
             attend_slots(t, 4, 6)
+            attend_slots(t, 2, 3)
             for i in pieces:
                 arrive(i, SAME[3] + 1)
-                arrive(i, SAME[2] + 1)
-            attend_slots(t, 0, 4)
+            attend_slots(t, 3, 4)
         else:
             attend_slots(t, 0, 6)
         span = pl.ds(t * rows, rows)

time: 76.1 us -> 76 us (level)
  no operation moved by 1% of the time
where the time goes in v5:
time: 76 us; the launch traced here: 75.8 us
  Pallas kernels  74 us (97%)
  local copies, waits for them, and re-layouts  1.87 us (2%)
    pallas_call x1, Pallas kernels, shards(): pl.pallas_call(functools.partial(kernel, chips, planes), out_shape=jax.Sh...  74 us
    unnamed x1, local copies, waits for them, and re-layouts  1.87 us

profile of v5, /device:TPU:1, one launch (start us, length us, event | category | flops | bytes accessed | tf_op | source)
XLA Modules:
  0.0 75.8 jit_solution(4050894383440242743)
XLA Ops:
  0.0 74.0 %shard_map.55 = bf16[512,512]{1,0:T(8,128)(2,1)} custom-call(s32[1,64]{1,0:T(1,128)} %bitcast.1, bf16[512,512]{1,0:T(8,128)(2,1)} %q_hbm.1, bf16[512,128]{1,0:T(8,128)(2,1)} %k_hbm.1, bf16[512,128]{1,0:T(8,128)(2,1)} %v_hbm.1, bf16[4096,512]{1,0:T(8,128)(2,1)} %w_hbm.1), custom_call_target="tpu_custom_call" | custom-call | tf_op jit(solution)/shard_map/pallas_call | solution.py:277
  74.0 1.9 %copy.7 = bf16[512,512]{1,0:T(8,128)(2,1)} copy(bf16[512,512]{1,0:T(8,128)(2,1)} %shard_map.55) | data formatting | bytes 1048576
